TPU v7x, 512 devices: a whole 4x8x8 slice. The times are simulated.
512 devices in a mesh: batch: 32 (over x, y), feat: 16 (over z, core).
Axes of the slice: x: 4, y: 8, z: 8, core: 2. Of those that a mesh axis runs over, the one named last changes fastest.
Arguments:
- view_one: bfloat16 [8192, 4096], P('batch', 'feat'), may hold values from -200 to 200
- view_two: bfloat16 [8192, 4096], P('batch', 'feat'), may hold values from -200 to 200
Outputs:
- total_loss: float32 [], replicated
- grad_one: bfloat16 [8192, 4096], P('batch', 'feat')
- grad_two: bfloat16 [8192, 4096], P('batch', 'feat')
All inputs are finite; a program needn't handle non-finite values.
Results may differ from a plain program's by a relative error of at most 0.017.
Values may be sent and summed in bfloat16 or wider, within the bound.
A program may use at most 64 MiB of HBM per device.

v0:
```python
import jax
import jax.numpy as jnp
from jax import lax
from jax.sharding import PartitionSpec as P

OFF_WEIGHT = 0.0051
EPSILON = 1e-05
LOSS_SCALE = 16.0


def on_device(view_one, view_two):
    row_count, col_width = view_one.shape
    batches = lax.axis_size("batch")
    groups = lax.axis_size("feat")
    sub_rows = col_width // batches
    full_width = col_width * groups
    row_total = row_count * batches
    first_float = view_one.astype(jnp.float32)
    second_float = view_two.astype(jnp.float32)
    moments = lax.psum(
        (
            jnp.sum(first_float, axis=0),
            jnp.sum(first_float * first_float, axis=0),
            jnp.sum(second_float, axis=0),
            jnp.sum(second_float * second_float, axis=0),
        ),
        "batch",
    )

    def finish(running, squares, data):
        center = running / row_total
        deviation = jnp.sqrt(squares / row_total - center * center + EPSILON)
        return (((data - center) / deviation).astype(jnp.bfloat16), deviation)

    norm_one, dev_one = finish(moments[0], moments[1], first_float)
    norm_two, dev_two = finish(moments[2], moments[3], second_float)
    partial_value = lax.dot_general(
        lax.all_gather(norm_two, "feat", axis=1, tiled=True),
        norm_one,
        (((0,), (0,)), ((), ())),
        preferred_element_type=jnp.float32,
    )
    partial_value = partial_value.reshape(groups, batches, sub_rows, col_width)
    corr_tile = (
        lax.psum_scatter(partial_value, "batch", scatter_dimension=1, tiled=True)[:, 0] / row_total
    )
    feat_index = lax.axis_index("feat")
    batch_index = lax.axis_index("batch")
    group_ids = lax.broadcasted_iota(jnp.int32, corr_tile.shape, 0)
    sub_ids = lax.broadcasted_iota(jnp.int32, corr_tile.shape, 1)
    col_ids = lax.broadcasted_iota(jnp.int32, corr_tile.shape, 2)
    on_diagonal = (group_ids == feat_index) & (col_ids == batch_index * sub_rows + sub_ids)
    local_loss = jnp.sum(
        jnp.where(on_diagonal, (1.0 - corr_tile) ** 2, OFF_WEIGHT * corr_tile * corr_tile)
    )
    total_loss = lax.psum(local_loss, ("batch", "feat"))
    grad_tile = jnp.where(
        on_diagonal, -2.0 * (1.0 - corr_tile), 2.0 * OFF_WEIGHT * corr_tile
    ).astype(jnp.bfloat16)
    cols_panel = lax.all_gather(grad_tile, "batch", axis=1, tiled=True).reshape(
        full_width, col_width
    )
    swapped = lax.all_to_all(grad_tile, "feat", split_axis=0, concat_axis=2, tiled=True)
    rows_panel = lax.all_gather(swapped, "batch", axis=1, tiled=True).reshape(col_width, full_width)
    panel_part = rows_panel
    dnorm_two = lax.dot_general(
        lax.all_gather(norm_one, "feat", axis=1, tiled=True),
        panel_part,
        (((1,), (1,)), ((), ())),
        preferred_element_type=jnp.float32,
    )
    panel_part = cols_panel
    dnorm_one = jnp.dot(
        lax.all_gather(norm_two, "feat", axis=1, tiled=True),
        panel_part,
        preferred_element_type=jnp.float32,
    )
    first_norm = norm_one.astype(jnp.float32)
    second_norm = norm_two.astype(jnp.float32)
    trace_one, trace_two = lax.psum(
        (
            jnp.sum(first_norm * dnorm_one, axis=0) / row_total,
            jnp.sum(second_norm * dnorm_two, axis=0) / row_total,
        ),
        "batch",
    )
    grad_one = (LOSS_SCALE * (dnorm_one - first_norm * trace_one) / dev_one).astype(jnp.bfloat16)
    grad_two = (LOSS_SCALE * (dnorm_two - second_norm * trace_two) / dev_two).astype(jnp.bfloat16)
    return (total_loss, grad_one, grad_two)


def solution(mesh):
    in_specs = (P("batch", "feat"), P("batch", "feat"))
    out_specs = (P(), P("batch", "feat"), P("batch", "feat"))
    return jax.shard_map(
        on_device, mesh=mesh, in_specs=in_specs, out_specs=out_specs, check_vma=False
    )
```

profile of v0, /device:TPU:64, one launch (start us, length us, event | category | flops | bytes accessed | tf_op | source)
XLA Modules:
  0.0 600.8 jit_solution(9506102930098437162)
XLA Ops:
  7.2 0.0 all-gather.5.cloned.1.call-start
  7.2 1.1 convert_reduce_fusion
  8.3 75.3 %all-reduce.2 = (f32[256]{0:T(256)S(1)}, f32[256]{0:T(256)S(1)}, f32[256]{0:T(256)S(1)}, f32[256]{0:T(256)S(1)}) all-reduce(f32[256]{0:T(256)S(1)} %get-tuple-element.23, f32[256]{0:T(256)S(1)} %get-tuple-element.24, f32[256]{0:T(256)S(1)} %get-tuple-element.4, ...), channel_id=1, replica_groups=mesh['batch'=32,'feat'=16] {'batch'}, use_global_device_ids=true, to_apply=%region_3.0 | all-reduce | flops 1024 | bytes 8192 | tf_op jit(solution)/shard_map/psum | solution.py:20
  83.6 1.6 fusion.11
  85.2 0.0 all-gather.5.cloned.1.call-update
  85.2 0.0 all-reduce.5.cloned.1.call-start
  85.2 0.9 fusion.14
  86.2 0.0 copy-start.1
  86.2 39.3 %all-gather.5.cloned.1.call-done = bf16[256,4096]{1,0:T(8,128)(2,1)} async-done(((bf16[256,256]{1,0:T(8,128)(2,1)}), bf16[256,4096]{1,0:T(8,128)(2,1)}) %all-gather.5.cloned.1.call-update) | async-done | bytes 2097168 | tf_op jit(solution)/shard_map/all_gather | solution.py:38
  125.5 4.3 fusion.23
  129.8 0.0 copy-done.1
  129.8 0.0 copy-start
  129.8 0.0 copy-start.2
  129.8 0.0 all-reduce.5.cloned.1.call-update
  129.9 0.0 all-gather.7.cloned.1.call-start
  129.9 1.4 dynamic-slice
  131.3 172.8 %all-reduce.5.cloned.1.call-done = f32[16,32,8,256]{3,2,1,0:T(8,128)} async-done(((f32[16,32,8,256]{3,2,1,0:T(8,128)}), f32[16,32,8,256]{3,2,1,0:T(8,128)}) %all-reduce.5.cloned.1.call-update) | async-done | bytes 4194320
  304.2 2.9 fusion.18
  307.0 0.0 all-gather.7.cloned.1.call-update
  307.1 0.0 all-gather.9.cloned.1.call-start
  307.1 0.5 all-gather.9.cloned.1.call-update
  307.6 0.0 all-gather.11.cloned.1.call-start
  307.7 14.4 %all_to_all.18 = bf16[16,8,256]{2,1,0:T(8,128)(2,1)} all-to-all(bf16[16,8,256]{2,1,0:T(8,128)(2,1)} %get-tuple-element.13), channel_id=1, replica_groups=mesh['batch'=32,'feat'=16] {'feat'}, dimensions={0} | all-to-all | bytes 131072 | tf_op jit(solution)/shard_map/all_to_all | solution.py:63
  322.1 0.0 all-gather.11.cloned.1.call-update
  322.1 96.1 %psum.53 = f32[]{:T(128)} all-reduce(f32[]{:T(128)} %get-tuple-element.14), channel_id=1, replica_groups=mesh['batch'=32,'feat'=16] {'batch','feat'}, use_global_device_ids=true, to_apply=%region_10.11 | all-reduce | flops 1 | bytes 8 | tf_op jit(solution)/shard_map/psum | solution.py:56
  418.2 0.0 all-gather.7.cloned.1.call-done
  418.2 0.0 copy-done
  418.2 0.0 copy-done.2
  418.2 0.0 copy-start.5
  418.2 2.4 fusion.2
  420.6 0.0 copy-start.3
  420.6 0.0 copy-start.4
  420.7 11.4 %all-gather.9.cloned.1.call-done = bf16[256,4096]{1,0:T(8,128)(2,1)} async-done(((bf16[256,256]{1,0:T(8,128)(2,1)}), bf16[256,4096]{1,0:T(8,128)(2,1)}) %all-gather.9.cloned.1.call-update) | async-done | bytes 2097168 | tf_op jit(solution)/shard_map/all_gather | solution.py:67
  432.0 85.9 %all-gather.11.cloned.1.call-done = bf16[1,256,4096]{2,1,0:T(8,128)(2,1)} async-done(((bf16[1,8,4096]{2,1,0:T(8,128)(2,1)}), bf16[1,256,4096]{2,1,0:T(8,128)(2,1)}) %all-gather.11.cloned.1.call-update) | async-done | bytes 2097168 | tf_op jit(solution)/shard_map/all_gather | solution.py:64
  517.9 0.0 copy-done.5
  517.9 3.0 fusion.6
  520.9 71.9 %all-reduce.1 = (f32[256]{0:T(256)S(1)}, f32[256]{0:T(256)S(1)}) all-reduce(f32[256]{0:T(256)S(1)} %broadcast_multiply_fusion.1, f32[256]{0:T(256)S(1)} %broadcast_multiply_fusion), channel_id=1, replica_groups=mesh['batch'=32,'feat'=16] {'batch'}, use_global_device_ids=true, to_apply=%region_12.13 | all-reduce | flops 512 | bytes 4096 | tf_op jit(solution)/shard_map/psum | solution.py:80
  592.8 0.0 copy-done.3
  592.8 0.7 fusion.16
  593.5 0.0 copy-done.4
  593.5 0.7 fusion.17
  (6 shorter events, 0.0 us)
Async XLA Ops:
  7.2 118.3 %all-gather.5.cloned.1.call-start = ((), (), s32[]{:S(2)}) async-start(), calls=%async_computation.1 | async-start | bytes 2228224 | tf_op jit(solution)/shard_map/all_gather | solution.py:38
  85.2 219.0 %all-reduce.5.cloned.1.call-start = ((), (), s32[]{:S(2)}) async-start(), calls=%async_computation.5 | async-start | bytes 8388608
  86.2 43.6 %copy-start.1 = (bf16[256,256]{1,0:T(8,128)(2,1)}, bf16[256,256]{1,0:T(8,128)(2,1)S(1)}, u32[]{:S(2)}) copy-start(bf16[256,256]{1,0:T(8,128)(2,1)S(1)} %fusion.14) | copy-start | bytes 393220
  129.8 288.4 %copy-start = (bf16[256,4096]{1,0:T(8,128)(2,1)S(1)}, bf16[256,4096]{1,0:T(8,128)(2,1)}, u32[]{:S(2)}) copy-start(bf16[256,4096]{1,0:T(8,128)(2,1)} %all-gather.5.cloned.1.call-done) | copy-start | bytes 6291460
  129.8 288.4 %copy-start.2 = (bf16[256,256]{1,0:T(8,128)(2,1)S(1)}, bf16[256,256]{1,0:T(8,128)(2,1)}, u32[]{:S(2)}) copy-start(bf16[256,256]{1,0:T(8,128)(2,1)} %copy-done.1) | copy-start | bytes 393220
  129.9 288.3 %all-gather.7.cloned.1.call-start = ((), (), s32[]{:S(2)}) async-start(), calls=%async_computation.2 | async-start | bytes 2162688 | tf_op jit(solution)/shard_map/all_gather | solution.py:60
  307.1 125.0 %all-gather.9.cloned.1.call-start = ((), (), s32[]{:S(2)}) async-start(), calls=%async_computation.3 | async-start | bytes 2228224 | tf_op jit(solution)/shard_map/all_gather | solution.py:67
  307.6 210.2 %all-gather.11.cloned.1.call-start = ((), (), s32[]{:S(2)}) async-start(), calls=%async_computation.4 | async-start | bytes 2162688 | tf_op jit(solution)/shard_map/all_gather | solution.py:64
  418.2 99.7 %copy-start.5 = (bf16[256,256]{1,0:T(8,128)(2,1)S(1)}, bf16[256,256]{1,0:T(8,128)(2,1)}, u32[]{:S(2)}) copy-start(bf16[256,256]{1,0:T(8,128)(2,1)} %fusion.11) | copy-start | bytes 393220
  420.6 172.2 %copy-start.3 = (bf16[256,256]{1,0:T(8,128)(2,1)S(1)}, bf16[256,256]{1,0:T(8,128)(2,1)}, u32[]{:S(2)}) copy-start(bf16[256,256]{1,0:T(8,128)(2,1)} %param.3) | copy-start | bytes 393220
  420.6 172.9 %copy-start.4 = (bf16[256,256]{1,0:T(8,128)(2,1)S(1)}, bf16[256,256]{1,0:T(8,128)(2,1)}, u32[]{:S(2)}) copy-start(bf16[256,256]{1,0:T(8,128)(2,1)} %param.2) | copy-start | bytes 393220
Sparse Core Ops, SparseCore 0:
  85.3 40.1 all-gather.4
  130.0 174.1 all-reduce.4
  307.7 77.9 all-gather.6
  388.3 43.6 all-gather.8
  435.5 82.3 all-gather.10
where the time goes:
time: 601 us
  waiting for transfers between devices  310 us (52%)
  blocking collectives  258 us (43%)
  between operations  13.9 us (2%)
  matrix products  9.71 us (2%)
  other arithmetic  7.95 us (1%)
    unnamed x6, waiting for transfers between devices  173 us
    psum x1, blocking collectives, on_device(): total_loss = lax.psum(local_loss, ('batch', 'feat'))  96.1 us
    all_gather x1, waiting for transfers between devices, on_device(): lax.all_gather(swapped, 'batch', axis=1, tiled=True)  85.9 us
    psum x1, blocking collectives, on_device(): lax.psum((jnp.sum(first_float, axis=0), jnp.sum(first_float * first_float...  75.3 us
    psum x1, blocking collectives, on_device(): lax.psum((jnp.sum(first_norm * dnorm_one, axis=0) / row_total, jnp.sum(se...  71.9 us
    all_gather x1, waiting for transfers between devices, on_device(): lax.all_gather(norm_two, 'feat', axis=1, tiled=True)  39.3 us
    all_to_all x1, blocking collectives, on_device(): lax.all_to_all(grad_tile, 'feat', split_axis=0, concat_axis=2, tiled=True)  14.4 us
  transfers between devices with their start and end apart: 5, of which 4 were waited for; matrix products, arithmetic and copies ran while one was open for 1% of the time, Pallas kernels for 0%

commit v1 on v0

v1 whole, which is shorter than its diff:
```python
import functools

import jax
import jax.numpy as jnp
from jax import lax
from jax.experimental import pallas as pl
from jax.experimental.pallas import tpu as pltpu
from jax.sharding import PartitionSpec as P

OFF_WEIGHT = 0.0051
EPSILON = 1e-05
LOSS_SCALE = 16.0
MESH = pl.DeviceIdType.MESH
F32 = jnp.float32
BF16 = jnp.bfloat16
STREAMS = 2
EXTRA = 16


def split_rows(values, width):
    row_ids = lax.broadcasted_iota(jnp.int32, (EXTRA, width), 0)
    block = jnp.zeros((EXTRA, width), F32)
    for k, value in enumerate(values):
        rest = value
        for part in range(3):
            piece = rest.astype(BF16).astype(F32)
            rest = rest - piece
            block = jnp.where(row_ids == 3 * k + part, piece, block)
    return block.astype(BF16)


def join_rows(block, count):
    wide = block.astype(F32)
    return [wide[3 * k : 3 * k + 1] + wide[3 * k + 1 : 3 * k + 2] + wide[3 * k + 2 : 3 * k + 3] for k in range(count)]


def stack_rows(values, width):
    row_ids = lax.broadcasted_iota(jnp.int32, (8, width), 0)
    block = jnp.zeros((8, width), F32)
    for k, value in enumerate(values):
        block = jnp.where(row_ids == k, value, block)
    return block


def kernel(
    xs, n, v1, v2, loss_o, g1_o, g2_o,
    raw1, raw2, n1f, n2f, own1, own2,
    st_a, st_b, st_xr, st_yr, tst_s, tst_r, sst_s, sst_r,
    acc, pst, pr, gx, gfull, sib_s, sib_r,
    rs_s, rs_r, ti_s, ti_r, ls_s, ls_r,
    t_sem, stx_sem, sty_sem, tst_sem, sst_sem, ag_ss, ag_rs, sb_ss, sb_rs,
    px_sem, gx_sem, sib_sem, rs_ss, rs_rs, ti_sem, ls_sem,
):
    rows, width = v1.shape
    half = n // 2
    srow = rows // STREAMS
    prow = width // xs
    total_rows = float(rows * n * xs)
    b, f = lax.axis_index("batch"), lax.axis_index("feat")
    x, y = lax.div(b, n), lax.rem(b, n)
    z, c = lax.div(f, 2), lax.rem(f, 2)
    o = 1 - c

    def dev(x_, y_, z_, c_):
        return (x_ * n + y_, z_ * 2 + c_)

    def wrap(v, m):
        return lax.rem(v + m, m)

    sibling = dev(x, y, z, o)
    partner = dev(x, z, y, c)
    x_peers = [dev(wrap(x + k, xs), y, z, c) for k in range(1, xs)]
    y_peers = [dev(x, wrap(y + k, n), z, c) for k in range(1, n)]
    ring = [
        [dev(x, wrap(y + 1, n), z, c), dev(x, wrap(y - 1, n), z, c)],
        [dev(x, y, wrap(z + 1, n), c), dev(x, y, wrap(z - 1, n), c)],
    ]
    pos = [y, z]
    off_diag = y != z
    on_diag = y == z

    def remote(src, dst, ss, rs, to):
        return pltpu.make_async_remote_copy(
            src_ref=src, dst_ref=dst, send_sem=ss, recv_sem=rs, device_id=to, device_id_type=MESH
        )

    barrier = pltpu.get_barrier_semaphore()
    greet = [sibling] + x_peers + y_peers + ring[1]
    for peer in greet:
        pl.semaphore_signal(barrier, inc=1, device_id=peer, device_id_type=MESH)

    @pl.when(off_diag)
    def _():
        pl.semaphore_signal(barrier, inc=1, device_id=partner, device_id_type=MESH)
        pl.semaphore_wait(barrier, len(greet) + 1)

    @pl.when(on_diag)
    def _():
        pl.semaphore_wait(barrier, len(greet))

    class Swap:
        def __init__(self, src, dst, sems):
            self.far = remote(src, dst, sems.at[0], sems.at[1], partner)
            self.near = pltpu.make_async_copy(src, dst, sems.at[1])

        def start(self):
            @pl.when(off_diag)
            def _():
                self.far.start()

            @pl.when(on_diag)
            def _():
                self.near.start()

        def wait_recv(self):
            @pl.when(off_diag)
            def _():
                self.far.wait_recv()

            @pl.when(on_diag)
            def _():
                self.near.wait()

        def wait_send(self):
            @pl.when(off_diag)
            def _():
                self.far.wait_send()

    swap = Swap(v2, raw2.at[c, y], t_sem)
    swap.start()
    late = []

    first, second = v1[...].astype(F32), v2[...].astype(F32)
    st_a[...] = stack_rows(
        [
            jnp.sum(first, axis=0, keepdims=True),
            jnp.sum(first * first, axis=0, keepdims=True),
            jnp.sum(second, axis=0, keepdims=True),
            jnp.sum(second * second, axis=0, keepdims=True),
        ],
        width,
    )
    stx = [remote(st_a, st_xr.at[k], stx_sem.at[0, k], stx_sem.at[1, k], to) for k, to in enumerate(x_peers)]
    for cp in stx:
        cp.start()

    def sib_copy(a, src, block, s, slot):
        sub = pl.ds(s * srow, srow)
        raw = (raw1, raw2)[a]
        return remote(src, raw.at[c, block, sub], sb_ss.at[a, slot, s], sb_rs.at[a, slot, s], sibling)

    def sib_recv(a, block, s, slot):
        sub = pl.ds(s * srow, srow)
        raw = (raw1, raw2)[a]
        return remote(raw.at[o, block, sub], raw.at[o, block, sub], sb_ss.at[a, slot, s], sb_rs.at[a, slot, s], sibling)

    for s in range(STREAMS):
        cp = sib_copy(0, v1.at[pl.ds(s * srow, srow)], y, s, 0)
        cp.start()
        late.append(cp)

    for cp in stx:
        cp.wait_recv()
    sums = st_a[...]
    for k in range(xs - 1):
        sums = sums + st_xr[k]
    st_b[...] = sums
    sty = [remote(st_b, st_yr.at[k], sty_sem.at[0, k], sty_sem.at[1, k], to) for k, to in enumerate(y_peers)]
    for cp in sty:
        cp.start()
    for cp in sty:
        cp.wait_recv()
    sums = st_b[...]
    for k in range(n - 1):
        sums = sums + st_yr[k]
    mean1, mean2 = sums[0:1] / total_rows, sums[2:3] / total_rows
    inv1 = 1.0 / jnp.sqrt(sums[1:2] / total_rows - mean1 * mean1 + EPSILON)
    inv2 = 1.0 / jnp.sqrt(sums[3:4] / total_rows - mean2 * mean2 + EPSILON)
    tst_s[...] = stack_rows([mean2, inv2], width)
    swap_st = Swap(tst_s, tst_r, tst_sem)
    swap_st.start()
    late += stx + sty

    def depth(d, s):
        return half if (s < STREAMS // 2) == (d == 0) else half - 1

    def ring_block(a, d, t):
        return wrap(pos[a] - t, n) if d == 0 else wrap(pos[a] + t, n)

    def ag_copy(a, d, t, s):
        sub = pl.ds(s * srow, srow)
        raw = (raw1, raw2)[a]
        block = ring_block(a, d, t)
        src = v1.at[sub] if (a == 0 and t == 0) else raw.at[c, block, sub]
        return remote(src, raw.at[c, block, sub], ag_ss.at[a, d, t, s], ag_rs.at[a, d, t, s], ring[a][d])

    for s in range(STREAMS):
        for d in range(2):
            if depth(d, s) > 0:
                cp = ag_copy(0, d, 0, s)
                cp.start()
                late.append(cp)
    own1[...] = ((first - mean1) * inv1).astype(BF16)
    own2[...] = ((second - mean2) * inv2).astype(BF16)
    swap.wait_recv()
    for s in range(STREAMS):
        for d in range(2):
            if depth(d, s) > 0:
                cp = ag_copy(1, d, 0, s)
                cp.start()
                late.append(cp)
        cp = sib_copy(1, raw2.at[c, z, pl.ds(s * srow, srow)], z, s, 0)
        cp.start()
        late.append(cp)

    def ring_slot(d, t):
        return 1 + t if d == 0 else 1 + half + t

    def forward(t):
        for s in range(STREAMS):
            for a in range(2):
                for d in range(2):
                    if t >= depth(d, s):
                        continue
                    ag_copy(a, d, t, s).wait_recv()
                    if t + 1 < depth(d, s):
                        cp = ag_copy(a, d, t + 1, s)
                        cp.start()
                        late.append(cp)
                    block = ring_block(a, d, t + 1)
                    cp = sib_copy(a, (raw1, raw2)[a].at[c, block, pl.ds(s * srow, srow)], block, s, ring_slot(d, t))
                    cp.start()
                    late.append(cp)

    forward(0)
    swap_st.wait_recv()
    mean2t, inv2t = tst_r[0:1], tst_r[1:2]
    sst_s[...] = stack_rows([mean1, inv1, mean2t, inv2t], width)
    sib_st = remote(sst_s, sst_r, sst_sem.at[0], sst_sem.at[1], sibling)
    sib_st.start()
    late.append(sib_st)
    for t in range(1, half):
        forward(t)
    sib_st.wait_recv()
    for a in range(2):
        for s in range(STREAMS):
            sib_recv(a, wrap(pos[a], n), s, 0).wait_recv()
            for d in range(2):
                for t in range(depth(d, s)):
                    sib_recv(a, ring_block(a, d, t + 1), s, ring_slot(d, t)).wait_recv()

    raw1[c, y] = v1[...]
    acc[...] = jnp.zeros_like(acc)

    def standard(i, _):
        n1f[c, i] = ((raw1[c, i].astype(F32) - mean1) * inv1).astype(BF16)
        n1f[o, i] = ((raw1[o, i].astype(F32) - sst_r[0:1]) * sst_r[1:2]).astype(BF16)
        n2f[c, i] = ((raw2[c, i].astype(F32) - mean2t) * inv2t).astype(BF16)
        n2f[o, i] = ((raw2[o, i].astype(F32) - sst_r[2:3]) * sst_r[3:4]).astype(BF16)
        for h in range(2):
            acc[h] += lax.dot_general(n1f[c, i], n2f[h, i], (((0,), (0,)), ((), ())), preferred_element_type=F32)
        return 0

    lax.fori_loop(0, n, standard, 0)

    row_ids = lax.broadcasted_iota(jnp.int32, (width, width), 0)
    col_ids = lax.broadcasted_iota(jnp.int32, (width, width), 1)
    diag_here = jnp.where(on_diag, 1.0, 0.0).astype(F32) / total_rows
    diag = jnp.sum(jnp.where(row_ids == col_ids, acc[c], 0.0), axis=0, keepdims=True) * diag_here
    extra = split_rows([diag], width)
    for k in range(xs):
        for h in range(2):
            pst[k, h, :prow] = (acc[h, k * prow : (k + 1) * prow] / total_rows).astype(BF16)
        pst[k, 0, prow:] = extra
        pst[k, 1, prow:] = extra
    px = [
        remote(pst.at[wrap(x + k, xs)], pr.at[k - 1], px_sem.at[0, k - 1], px_sem.at[1, k - 1], x_peers[k - 1])
        for k in range(1, xs)
    ]
    for cp in px:
        cp.start()
    late += px
    for cp in px:
        cp.wait_recv()
    for k in range(xs - 1):
        diag = diag + join_rows(pr[k, 0, prow:], 1)[0]
    diag_grad = (-2.0 * (1.0 - diag)).astype(BF16).astype(F32) * jnp.where(on_diag, 1.0, 0.0).astype(F32)
    prow_ids = lax.broadcasted_iota(jnp.int32, (prow, width), 0) + x * prow
    pcol_ids = lax.broadcasted_iota(jnp.int32, (prow, width), 1)
    same = prow_ids == pcol_ids
    loss = jnp.zeros((1, 1), F32)
    row_trace = jnp.zeros((prow, 1), F32)
    col_trace = []
    for h in range(2):
        corr = acc[h, pl.ds(pl.multiple_of(x * prow, prow), prow)] / total_rows
        for k in range(xs - 1):
            corr = corr + pr[k, h, :prow].astype(F32)
        spot = same & on_diag & (c == h)
        terms = jnp.where(spot, (1.0 - diag) * (1.0 - diag), OFF_WEIGHT * corr * corr)
        loss = loss + jnp.sum(jnp.sum(terms, axis=0, keepdims=True), axis=1, keepdims=True)
        grad = jnp.where(spot, 0.0, 2.0 * OFF_WEIGHT * corr).astype(BF16)
        gx[x, h, :prow] = grad
        share = corr * grad.astype(F32)
        row_trace = row_trace + jnp.sum(share, axis=1, keepdims=True)
        col_trace.append(jnp.sum(share, axis=0, keepdims=True))
    row_trace = jnp.sum(jnp.where(same, row_trace, 0.0), axis=0, keepdims=True)
    loss_row = jnp.zeros((1, width), F32) + loss
    gx[x, 0, prow:] = split_rows([col_trace[0], row_trace, loss_row], width)
    gx[x, 1, prow:] = split_rows([col_trace[1]], width)
    gc = [remote(gx.at[x], gx.at[x], gx_sem.at[0, k], gx_sem.at[1, k], to) for k, to in enumerate(x_peers)]
    for cp in gc:
        cp.start()
    for cp in late:
        cp.wait_send()
    swap.wait_send()
    swap_st.wait_send()
    for k in range(1, xs):
        src = wrap(x - k, xs)
        remote(gx.at[src], gx.at[src], gx_sem.at[0, k - 1], gx_sem.at[1, k - 1], x_peers[k - 1]).wait_recv()
    col0 = col1 = trace1 = loss_row = jnp.zeros((1, width), F32)
    for k in range(xs):
        for h in range(2):
            gfull[h, k * prow : (k + 1) * prow] = gx[k, h, :prow]
        part = join_rows(gx[k, 0, prow:], 3)
        col0, trace1, loss_row = col0 + part[0], trace1 + part[1], loss_row + part[2]
        col1 = col1 + join_rows(gx[k, 1, prow:], 1)[0]
    is_low = c == 0
    mine = jnp.where(is_low, col0, col1)
    theirs = jnp.where(is_low, col1, col0)
    diag_trace = diag * diag_grad
    trace1 = trace1 + diag_trace
    trace2 = mine + diag_trace

    sib_s[:width] = gfull[o]
    sib_s[width:] = split_rows([theirs, loss_row], width)
    sib = remote(sib_s, sib_r, sib_sem.at[0], sib_sem.at[1], sibling)
    sib.start()
    late = gc + [sib]
    sib.wait_recv()
    part = join_rows(sib_r[width:], 2)
    trace2 = trace2 + part[0]
    loss_row = loss_row + part[1]

    ring_extra = [[trace1, diag_grad], [trace2, loss_row]]

    def product(a, block, s):
        sub = pl.ds(s * srow, srow)
        if a == 0:
            dims = (((1,), (1,)), ((), ()))
            left, right = (n2f[0, block, sub], n2f[1, block, sub]), (gfull[0], gfull[1])
        else:
            dims = (((1,), (0,)), ((), ()))
            left, right = (n1f[c, block, sub], n1f[o, block, sub]), (gfull[c], sib_r[:width])
        return lax.dot_general(left[0], right[0], dims, preferred_element_type=F32) + lax.dot_general(
            left[1], right[1], dims, preferred_element_type=F32
        )

    def rs_copy(a, d, t, s):
        sub = pl.ds(0, srow + (EXTRA if s == 0 else 0))
        return remote(
            rs_s.at[a, d, t, s, sub], rs_r.at[a, d, t, s, sub], rs_ss.at[a, d, t, s], rs_rs.at[a, d, t, s], ring[a][d]
        )

    for t in range(half):
        for s in range(STREAMS):
            for a in range(2):
                for d in range(2):
                    deep = depth(d, s)
                    if t >= deep:
                        continue
                    block = ring_block(a, 1 - d, deep - t)
                    value = product(a, block, s)
                    if t > 0:
                        rs_copy(a, d, t - 1, s).wait_recv()
                        value = value + rs_r[a, d, t - 1, s, :srow].astype(F32)
                    rs_s[a, d, t, s, :srow] = value.astype(BF16)
                    if s == 0:
                        carried = ring_extra[a]
                        if t > 0:
                            got = join_rows(rs_r[a, d, t - 1, s, srow:], 2)
                            carried = [u + w for u, w in zip(carried, got)]
                        rs_s[a, d, t, s, srow:] = split_rows(carried, width)
                    cp = rs_copy(a, d, t, s)
                    cp.start()
                    late.append(cp)

    def finish(a, s):
        value = product(a, pos[a], s)
        carried = ring_extra[a]
        for d in range(2):
            deep = depth(d, s)
            if deep == 0:
                continue
            rs_copy(a, d, deep - 1, s).wait_recv()
            value = value + rs_r[a, d, deep - 1, s, :srow].astype(F32)
            if s == 0:
                got = join_rows(rs_r[a, d, deep - 1, s, srow:], 2)
                carried = [u + w for u, w in zip(carried, got)]
        return value, carried

    backs = []
    for s in range(STREAMS):
        value, carried = finish(1, s)
        ti_s[s, :srow] = value.astype(BF16)
        if s == 0:
            trace2, loss_row = carried
            ti_s[s, srow:] = split_rows([trace2], width)
        else:
            ti_s[s, srow:] = jnp.zeros((EXTRA, width), BF16)
        back = Swap(ti_s.at[s], ti_r.at[s], ti_sem.at[s])
        back.start()
        backs.append(back)
    ls_s[...] = jnp.zeros((8, width), F32) + loss_row
    lc = [remote(ls_s, ls_r.at[k], ls_sem.at[0, k], ls_sem.at[1, k], to) for k, to in enumerate(y_peers)]
    for cp in lc:
        cp.start()
    late += lc
    for s in range(STREAMS):
        value, carried = finish(0, s)
        if s == 0:
            trace1, diag_grad = carried
        sub = pl.ds(s * srow, srow)
        value = value + own2[sub].astype(F32) * diag_grad - own1[sub].astype(F32) * trace1
        g1_o[sub] = (LOSS_SCALE * value * inv1).astype(BF16)
    for cp in late:
        cp.wait_send()
    for cp in lc:
        cp.wait_recv()
    for k in range(n - 1):
        loss_row = loss_row + ls_r[k, 0:1]
    loss_o[...] = loss_row[:, 0:1]
    for s in range(STREAMS):
        backs[s].wait_recv()
        if s == 0:
            trace2 = join_rows(ti_r[0, srow:], 1)[0]
        sub = pl.ds(s * srow, srow)
        value = ti_r[s, :srow].astype(F32) + own1[sub].astype(F32) * diag_grad - own2[sub].astype(F32) * trace2
        g2_o[sub] = (LOSS_SCALE * value * inv2).astype(BF16)
    for back in backs:
        back.wait_send()


def on_device(xs, n, view_one, view_two):
    rows, width = view_one.shape
    half = n // 2
    srow = rows // STREAMS
    prow = width // xs
    sem = pltpu.SemaphoreType.DMA
    blocks = (2, n, rows, width)
    ring = (2, 2, half, STREAMS)
    loss, grad_one, grad_two = pl.pallas_call(
        functools.partial(kernel, xs, n),
        out_shape=(
            jax.ShapeDtypeStruct((1, 1), F32),
            jax.ShapeDtypeStruct((rows, width), BF16),
            jax.ShapeDtypeStruct((rows, width), BF16),
        ),
        in_specs=[pl.BlockSpec(memory_space=pltpu.VMEM)] * 2,
        out_specs=[pl.BlockSpec(memory_space=pltpu.VMEM)] * 3,
        scratch_shapes=[
            pltpu.VMEM(blocks, BF16),
            pltpu.VMEM(blocks, BF16),
            pltpu.VMEM(blocks, BF16),
            pltpu.VMEM(blocks, BF16),
            pltpu.VMEM((rows, width), BF16),
            pltpu.VMEM((rows, width), BF16),
            pltpu.VMEM((8, width), F32),
            pltpu.VMEM((8, width), F32),
            pltpu.VMEM((xs - 1, 8, width), F32),
            pltpu.VMEM((n - 1, 8, width), F32),
            pltpu.VMEM((8, width), F32),
            pltpu.VMEM((8, width), F32),
            pltpu.VMEM((8, width), F32),
            pltpu.VMEM((8, width), F32),
            pltpu.VMEM((2, width, width), F32),
            pltpu.VMEM((xs, 2, prow + EXTRA, width), BF16),
            pltpu.VMEM((xs - 1, 2, prow + EXTRA, width), BF16),
            pltpu.VMEM((xs, 2, prow + EXTRA, width), BF16),
            pltpu.VMEM((2, width, width), BF16),
            pltpu.VMEM((width + EXTRA, width), BF16),
            pltpu.VMEM((width + EXTRA, width), BF16),
            pltpu.VMEM(ring + (srow + EXTRA, width), BF16),
            pltpu.VMEM(ring + (srow + EXTRA, width), BF16),
            pltpu.VMEM((STREAMS, srow + EXTRA, width), BF16),
            pltpu.VMEM((STREAMS, srow + EXTRA, width), BF16),
            pltpu.VMEM((8, width), F32),
            pltpu.VMEM((n - 1, 8, width), F32),
            sem((2,)),
            sem((2, xs - 1)),
            sem((2, n - 1)),
            sem((2,)),
            sem((2,)),
            sem(ring),
            sem(ring),
            sem((2, n + 1, STREAMS)),
            sem((2, n + 1, STREAMS)),
            sem((2, xs - 1)),
            sem((2, xs - 1)),
            sem((2,)),
            sem(ring),
            sem(ring),
            sem((STREAMS, 2)),
            sem((2, n - 1)),
        ],
        compiler_params=pltpu.CompilerParams(
            collective_id=0, has_side_effects=True, vmem_limit_bytes=40 * 2**20
        ),
        name="barlow",
    )(view_one, view_two)
    return loss.reshape(()), grad_one, grad_two


def solution(mesh):
    n = mesh.shape["feat"] // 2
    xs = mesh.shape["batch"] // n
    spec = P("batch", "feat")
    return jax.shard_map(
        functools.partial(on_device, xs, n),
        mesh=mesh,
        in_specs=(spec, spec),
        out_specs=(P(), spec, spec),
        check_vma=False,
    )
```

time: 601 us -> 106 us (0.18)
  the two profiles are of different devices: /device:TPU:64 before, /device:TPU:1 now
where the time goes in v1:
time: 106 us
  Pallas kernels  100 us (94%)
  local copies, waits for them, and re-layouts  3.11 us (3%)
  between operations  2.41 us (2%)
    pallas_call x1, Pallas kernels, on_device(): pl.pallas_call(functools.partial(kernel, xs, n), out_shape=(jax.ShapeDtyp...  100 us
    unnamed x6, local copies, waits for them, and re-layouts  3.11 us

profile of v1, /device:TPU:1, one launch (start us, length us, event | category | flops | bytes accessed | tf_op | source)
XLA Modules:
  0.0 105.5 jit_solution(3268970194663806798)
XLA Ops:
  0.6 0.0 copy-start
  0.6 0.9 copy-done
  1.5 0.0 copy-start.1
  1.5 0.9 copy-done.1
  2.4 100.0 %barlow.1 = (f32[1,1]{1,0:T(1,128)}, bf16[256,256]{1,0:T(8,128)(2,1)S(1)}, bf16[256,256]{1,0:T(8,128)(2,1)S(1)}) custom-call(bf16[256,256]{1,0:T(8,128)(2,1)S(1)} %copy-done, bf16[256,256]{1,0:T(8,128)(2,1)S(1)} %copy-done.1), custom_call_target="tpu_custom_call" | custom-call | tf_op jit(solution)/shard_map/barlow/pallas_call | solution.py:451
  103.1 0.7 copy.9
  103.8 0.7 copy.10
Async XLA Ops:
  0.6 0.9 copy-start
  1.5 0.9 copy-start.1

commit v2 on v1

v2 whole, which is shorter than its diff:
```python
import functools

import jax
import jax.numpy as jnp
from jax import lax
from jax.experimental import pallas as pl
from jax.experimental.pallas import tpu as pltpu
from jax.sharding import PartitionSpec as P

OFF_WEIGHT = 0.0051
EPSILON = 1e-05
LOSS_SCALE = 16.0
MESH = pl.DeviceIdType.MESH
F32 = jnp.float32
BF16 = jnp.bfloat16
STREAMS = 2
EXTRA = 16


def split_rows(values, width):
    row_ids = lax.broadcasted_iota(jnp.int32, (EXTRA, width), 0)
    block = jnp.zeros((EXTRA, width), F32)
    for k, value in enumerate(values):
        rest = value
        for part in range(3):
            piece = rest.astype(BF16).astype(F32)
            rest = rest - piece
            block = jnp.where(row_ids == 3 * k + part, piece, block)
    return block.astype(BF16)


def join_rows(block, count):
    wide = block.astype(F32)
    return [wide[3 * k : 3 * k + 1] + wide[3 * k + 1 : 3 * k + 2] + wide[3 * k + 2 : 3 * k + 3] for k in range(count)]


def stack_rows(values, width):
    row_ids = lax.broadcasted_iota(jnp.int32, (8, width), 0)
    block = jnp.zeros((8, width), F32)
    for k, value in enumerate(values):
        block = jnp.where(row_ids == k, value, block)
    return block


def kernel(
    xs, n, v1, v2, loss_o, g1_o, g2_o,
    raw1, raw2, n1f, n2f, own2, hop_a, hop_b, ssum, qsum, tst_s, tst_r, tr_s, tr_r,
    acc, pst, pr, gx, gfull, sib_s, sib_r,
    rs_s, rs_r, ti_s, ti_r, ls_s, ls_r,
    in_sem, t_sem, tst_sem, tr_sem, ag_ss, ag_rs, sb_ss, sb_rs,
    px_sem, gx_sem, sib_sem, rs_ss, rs_rs, ti_sem, ls_sem,
):
    rows, width = v1.shape
    half = n // 2
    srow = rows // STREAMS
    prow = width // xs
    part_rows = rows // n
    group_rows = float(rows * n)
    total_rows = float(rows * n * xs)
    b, f = lax.axis_index("batch"), lax.axis_index("feat")
    x, y = lax.div(b, n), lax.rem(b, n)
    z, c = lax.div(f, 2), lax.rem(f, 2)
    o = 1 - c
    is_low = c == 0
    skip = half == 4

    def dev(x_, y_, z_, c_):
        return (x_ * n + y_, z_ * 2 + c_)

    def wrap(v, m):
        return lax.rem(v + m, m)

    sibling = dev(x, y, z, o)
    partner = dev(x, z, y, c)
    x_peers = [dev(wrap(x + k, xs), y, z, c) for k in range(1, xs)]
    y_peers = [dev(x, wrap(y + k, n), z, c) for k in range(1, n)]
    z_peers = [dev(x, y, wrap(z + k, n), c) for k in range(1, n)]
    nearest = sorted(range(1, n), key=lambda k: min(k, n - k))

    def along(a, k):
        return dev(x, wrap(y + k, n), z, c) if a == 0 else dev(x, y, wrap(z + k, n), c)

    ring = [[along(a, 1), along(a, -1)] for a in range(2)]
    ring2 = [[along(a, 2), along(a, -2)] for a in range(2)] if skip else None
    pos = [y, z]
    off_diag = y != z
    on_diag = y == z
    diag_one = jnp.where(on_diag, 1.0, 0.0).astype(F32)

    def remote(src, dst, ss, rs, to):
        return pltpu.make_async_remote_copy(
            src_ref=src, dst_ref=dst, send_sem=ss, recv_sem=rs, device_id=to, device_id_type=MESH
        )

    def stream(s):
        return pl.ds(s * srow, srow)

    load1 = pltpu.make_async_copy(v1, raw1.at[c, y], in_sem.at[0])
    load2 = pltpu.make_async_copy(v2, own2, in_sem.at[1])
    load1.start()
    load2.start()
    barrier = pltpu.get_barrier_semaphore()
    greet = [sibling] + x_peers + y_peers + z_peers
    for peer in greet:
        pl.semaphore_signal(barrier, inc=1, device_id=peer, device_id_type=MESH)

    @pl.when(off_diag)
    def _():
        pl.semaphore_signal(barrier, inc=1, device_id=partner, device_id_type=MESH)

    load1.wait()
    load2.wait()

    @pl.when(off_diag)
    def _():
        pl.semaphore_wait(barrier, len(greet) + 1)

    @pl.when(on_diag)
    def _():
        pl.semaphore_wait(barrier, len(greet))

    class Swap:
        def __init__(self, src, dst, sems):
            self.far = remote(src, dst, sems.at[0], sems.at[1], partner)
            self.near = pltpu.make_async_copy(src, dst, sems.at[1])

        def start(self):
            @pl.when(off_diag)
            def _():
                self.far.start()

            @pl.when(on_diag)
            def _():
                self.near.start()

        def wait_recv(self):
            @pl.when(off_diag)
            def _():
                self.far.wait_recv()

            @pl.when(on_diag)
            def _():
                self.near.wait()

        def wait_send(self):
            @pl.when(off_diag)
            def _():
                self.far.wait_send()

    late = []

    def go(cp):
        cp.start()
        late.append(cp)

    def part(k):
        return pl.ds(pl.multiple_of(k * part_rows, part_rows), part_rows)

    class Exchange:
        def __init__(self, source, hop, target, sems, along_z):
            self.source, self.hop, self.target, self.sems = source, hop, target, sems
            self.peers = z_peers if along_z else y_peers
            self.here, self.there = (z, y) if along_z else (y, z)
            self.to = (lambda k: dev(x, k, z, c)) if along_z else (lambda k: dev(x, y, k, c))

        def first(self, k):
            hop_ref = self.hop.at[self.here]
            return remote(
                self.source(wrap(self.here + k, n)), hop_ref, self.sems.at[0, k], self.sems.at[1, k], self.peers[k - 1]
            )

        def stay(self):
            return pltpu.make_async_copy(self.source(self.here), self.hop.at[self.here], self.sems.at[1, 0])

        def second(self, k):
            origin = wrap(self.here - k, n)
            far = remote(
                self.hop.at[origin], self.target(self.there), self.sems.at[2, k], self.sems.at[3, self.there], self.to(origin)
            )
            near = pltpu.make_async_copy(self.hop.at[origin], self.target(self.there), self.sems.at[3, self.there])
            return origin, far, near

        def start(self):
            self.stay().start()
            for k in nearest:
                self.first(k).start()

        def pass_on(self, some):
            for k in some:
                if k == 0:
                    self.stay().wait()
                else:
                    self.first(k).wait_recv()
                origin, far, near = self.second(k)

                @pl.when(origin != self.there)
                def _():
                    far.start()

                @pl.when(origin == self.there)
                def _():
                    near.start()

        def wait_recv(self):
            for k in [0] + nearest:
                came = wrap(self.there + k, n)
                ref = self.target(came)
                if k == 0:
                    pltpu.make_async_copy(ref, ref, self.sems.at[3, came]).wait()
                else:
                    remote(ref, ref, self.sems.at[2, k], self.sems.at[3, came], self.peers[0]).wait_recv()

        def wait_send(self):
            for k in nearest:
                self.first(k).wait_send()
            for k in range(n):
                origin, far, _ = self.second(k)

                @pl.when(origin != self.there)
                def _():
                    far.wait_send()

    spread_out = Exchange(lambda k: own2.at[part(k)], hop_a, lambda k: raw2.at[c, k, part(z)], t_sem, True)
    spread_out.start()

    raws, norms = (raw1, raw2), (n1f, n2f)

    def depth(d, s):
        return half if (s < STREAMS // 2) == (d == 0) else half - 1

    def ring_block(a, d, t):
        return wrap(pos[a] - t, n) if d == 0 else wrap(pos[a] + t, n)

    def piece(a, core, block, s):
        if a == 0:
            return raw1.at[core, block, stream(s)]
        return raw2.at[core, pl.ds(s * n // STREAMS, n // STREAMS), part(block)]

    def block_of(refs, a, core, block):
        if a == 0:
            return refs[core, block]
        return refs[core, :, part(block)].reshape(rows, width)

    def ag_copy(a, d, t, s):
        far = skip and t == 3
        block = ring_block(a, d, 2 if far else t)
        ref = piece(a, c, block, s)
        return remote(ref, ref, ag_ss.at[a, d, t, s], ag_rs.at[a, d, t, s], (ring2 if far else ring)[a][d])

    def sib_copy(a, core, block, s, slot):
        ref = piece(a, core, block, s)
        return remote(ref, ref, sb_ss.at[a, slot, s], sb_rs.at[a, slot, s], sibling)

    def ring_slot(d, t):
        return 1 + t if d == 0 else 1 + half + t

    def open_ring(a, s):
        for d in range(2):
            if depth(d, s) > 0:
                go(ag_copy(a, d, 0, s))
        go(sib_copy(a, c, pos[a], s, 0))

    def forward(a, t):
        for s in range(STREAMS):
            for d in range(2):
                if t >= depth(d, s):
                    continue
                ag_copy(a, d, t, s).wait_recv()
                if t + 1 < min(depth(d, s), 3 if skip else half):
                    go(ag_copy(a, d, t + 1, s))
                if skip and t == 1 and depth(d, s) == 4:
                    go(ag_copy(a, d, 3, s))
                go(sib_copy(a, c, ring_block(a, d, t + 1), s, ring_slot(d, t)))

    def sib_wait(a, s, d, t):
        if d is None:
            sib_copy(a, o, pos[a], s, 0).wait_recv()
        elif t < depth(d, s):
            sib_copy(a, o, ring_block(a, d, t + 1), s, ring_slot(d, t)).wait_recv()

    shifts = {}

    def fold(value):
        return jnp.sum(value.reshape(rows // 8, 8, width), axis=0)

    def shifted(a, block, begin):
        for h, core in enumerate((c, o)):
            value = block_of(raws[a], a, core, block).astype(F32)
            if begin:
                shifts[a, h] = jnp.sum(fold(value), axis=0, keepdims=True) / rows
            value = value - shifts[a, h]
            if a == 0:
                norms[a][core, block] = value.astype(BF16)
            else:
                norms[a][core, :, part(block)] = value.astype(BF16).reshape(n, part_rows, width)
            if begin:
                ssum[a, h] = fold(value)
                qsum[a, h] = fold(value * value)
            else:
                ssum[a, h] += fold(value)
                qsum[a, h] += fold(value * value)

    def correlate(block, begin):
        for h in range(2):
            share = lax.dot_general(
                block_of(n1f, 1, c, block), block_of(n2f, 1, h, block), (((0,), (0,)), ((), ())), preferred_element_type=F32
            )
            if begin:
                acc[h] = share
            else:
                acc[h] += share

    def arrived(a, t):
        if t + 1 < half:
            blocks = [ring_block(a, 0, t + 1), ring_block(a, 1, t + 1)]
        else:
            blocks = [ring_block(a, 0, half)]
        for s in range(STREAMS):
            for d in range(2):
                sib_wait(a, s, d, t)
        for block in blocks:
            shifted(a, block, False)
            if a == 1:
                correlate(block, False)

    for s in range(STREAMS):
        open_ring(0, s)
    spread_out.pass_on([0] + nearest)
    spread_out.wait_recv()
    for s in range(STREAMS):
        open_ring(1, s)
    for s in range(STREAMS):
        sib_wait(0, s, None, 0)
    shifted(0, y, True)
    forward(0, 0)
    forward(1, 0)
    for s in range(STREAMS):
        sib_wait(1, s, None, 0)
    shifted(1, z, True)
    for t in range(1, half):
        forward(0, t)
        forward(1, t)
        arrived(0, t - 1)
        if t == 1 and half > 1:
            pass
    arrived(0, half - 1)
    correlate(z, True)
    for t in range(half):
        arrived(1, t)

    def spread(row, count, first):
        ids = lax.broadcasted_iota(jnp.int32, (count, width), 0) + first
        lanes = lax.broadcasted_iota(jnp.int32, (count, width), 1)
        return jnp.sum(jnp.where(ids == lanes, row, 0.0), axis=1, keepdims=True)

    rests, means, squares = {}, {}, {}
    for a in range(2):
        for h in range(2):
            rest = jnp.sum(ssum[a, h], axis=0, keepdims=True) / group_rows
            rests[a, h] = rest
            means[a, h] = shifts[a, h] + rest
            squares[a, h] = jnp.sum(qsum[a, h], axis=0, keepdims=True) - group_rows * rest * rest

    def by_half(table, a):
        return [jnp.where(is_low, table[a, 0], table[a, 1]), jnp.where(is_low, table[a, 1], table[a, 0])]

    rest2, mean2, square2 = by_half(rests, 1), by_half(means, 1), by_half(squares, 1)
    column = spread(rests[0, 0], width, 0) * (group_rows / total_rows)
    row_ids = lax.broadcasted_iota(jnp.int32, (width, width), 0)
    col_ids = lax.broadcasted_iota(jnp.int32, (width, width), 1)
    for h in range(2):
        acc[h] = acc[h] / total_rows - column * rest2[h]
    diag = jnp.sum(jnp.where(row_ids == col_ids, acc[c], 0.0), axis=0, keepdims=True) * diag_one
    facts = [
        [means[0, 0], squares[0, 0], mean2[0], square2[0], diag],
        [means[0, 1], squares[0, 1], mean2[1], square2[1]],
    ]

    for h in range(2):
        extra = split_rows(facts[h], width)
        for k in range(xs):
            pst[k, h, :prow] = acc[h, k * prow : (k + 1) * prow].astype(BF16)
            pst[k, h, prow:] = extra
    px = [
        remote(pst.at[wrap(x + k, xs)], pr.at[k - 1], px_sem.at[0, k - 1], px_sem.at[1, k - 1], x_peers[k - 1])
        for k in range(1, xs)
    ]
    for cp in px:
        go(cp)
    for cp in px:
        cp.wait_recv()
    every = [facts]
    for k in range(xs - 1):
        every.append([join_rows(pr[k, 0, prow:], 5), join_rows(pr[k, 1, prow:], 4)])

    def whole(h, place):
        center = sum(e[h][place] for e in every) / xs
        spreads = [e[h][place] - center for e in every]
        square = sum(e[h][place + 1] for e in every) + group_rows * sum(v * v for v in spreads)
        return center, 1.0 / jnp.sqrt(square / total_rows + EPSILON), spreads

    center1, inv1, spread1 = whole(0, 0)
    center1o, inv1o, _ = whole(1, 0)
    center2, inv2, spread2 = [[v[h] for h in range(2)] for v in zip(*[whole(h, 2) for h in range(2)])]
    near2 = [jnp.where(is_low, v[0], v[1]) for v in (center2, inv2)]
    near_spread2 = [jnp.where(is_low, u, w) for u, w in zip(*spread2)]
    tst_s[...] = stack_rows(near2, width)
    swap_st = Swap(tst_s, tst_r, tst_sem)
    swap_st.start()

    diag = sum(e[0][4] for e in every) + sum(u * w for u, w in zip(spread1, near_spread2)) / xs * diag_one
    diag = diag * inv1 * near2[1]
    diag_grad = (-2.0 * (1.0 - diag)).astype(BF16).astype(F32) * diag_one
    prow_ids = lax.broadcasted_iota(jnp.int32, (prow, width), 0) + x * prow
    pcol_ids = lax.broadcasted_iota(jnp.int32, (prow, width), 1)
    same = prow_ids == pcol_ids
    inv_column = spread(inv1, prow, x * prow)
    spread_columns = [spread(v, prow, x * prow) / xs for v in spread1]
    loss = jnp.zeros((1, 1), F32)
    row_trace = jnp.zeros((prow, 1), F32)
    col_trace = []
    for h in range(2):
        corr = acc[h, pl.ds(pl.multiple_of(x * prow, prow), prow)]
        for k in range(xs - 1):
            corr = corr + pr[k, h, :prow].astype(F32)
        for k in range(xs):
            corr = corr + spread_columns[k] * spread2[h][k]
        corr = corr * inv_column * inv2[h]
        spot = same & on_diag & (c == h)
        terms = jnp.where(spot, (1.0 - diag) * (1.0 - diag), OFF_WEIGHT * corr * corr)
        loss = loss + jnp.sum(jnp.sum(terms, axis=0, keepdims=True), axis=1, keepdims=True)
        grad = jnp.where(spot, 0.0, 2.0 * OFF_WEIGHT * corr).astype(BF16)
        gx[x, h, :prow] = grad
        share = corr * grad.astype(F32)
        row_trace = row_trace + jnp.sum(share, axis=1, keepdims=True)
        col_trace.append(jnp.sum(share, axis=0, keepdims=True))
    row_trace = jnp.sum(jnp.where(same, row_trace, 0.0), axis=0, keepdims=True)
    loss_row = jnp.zeros((1, width), F32) + loss
    gx[x, 0, prow:] = split_rows([col_trace[0], row_trace, loss_row], width)
    gx[x, 1, prow:] = split_rows([col_trace[1]], width)
    gc = [remote(gx.at[x], gx.at[x], gx_sem.at[0, k], gx_sem.at[1, k], to) for k, to in enumerate(x_peers)]
    for cp in gc:
        cp.start()

    def standard(i, _):
        n1f[c, i] = ((raw1[c, i].astype(F32) - center1) * inv1).astype(BF16)
        n1f[o, i] = ((raw1[o, i].astype(F32) - center1o) * inv1o).astype(BF16)
        for h in range(2):
            n2f[h, i] = ((raw2[h, i].astype(F32) - center2[h]) * inv2[h]).astype(BF16)
        return 0

    lax.fori_loop(0, n, standard, 0)
    for cp in late:
        cp.wait_send()
    spread_out.wait_send()
    swap_st.wait_send()
    for k in range(1, xs):
        src = wrap(x - k, xs)
        remote(gx.at[src], gx.at[src], gx_sem.at[0, k - 1], gx_sem.at[1, k - 1], x_peers[k - 1]).wait_recv()
    col0 = col1 = trace1 = loss_row = jnp.zeros((1, width), F32)
    for k in range(xs):
        for h in range(2):
            gfull[h, k * prow : (k + 1) * prow] = gx[k, h, :prow]
        got = join_rows(gx[k, 0, prow:], 3)
        col0, trace1, loss_row = col0 + got[0], trace1 + got[1], loss_row + got[2]
        col1 = col1 + join_rows(gx[k, 1, prow:], 1)[0]
    mine = jnp.where(is_low, col0, col1)
    theirs = jnp.where(is_low, col1, col0)
    diag_trace = diag * diag_grad
    trace1 = trace1 + diag_trace
    trace2 = mine + diag_trace

    sib_s[:width] = gfull[o]
    sib_s[width:] = split_rows([theirs, loss_row], width)
    sib = remote(sib_s, sib_r, sib_sem.at[0], sib_sem.at[1], sibling)
    sib.start()
    late = gc + [sib]
    sib.wait_recv()
    got = join_rows(sib_r[width:], 2)
    trace2 = trace2 + got[0]
    loss_row = loss_row + got[1]

    ring_extra = [[trace1, diag_grad], [trace2, loss_row]]

    def product(a, block, s):
        if a == 0:
            dims = (((1,), (1,)), ((), ()))
            left, right = [n2f[h, block, stream(s)] for h in range(2)], (gfull[0], gfull[1])
        else:
            dims = (((1,), (0,)), ((), ()))
            images = pl.ds(s * n // STREAMS, n // STREAMS)
            left = [n1f[h, images, part(block)].reshape(srow, width) for h in (c, o)]
            right = (gfull[c], sib_r[:width])
        return lax.dot_general(left[0], right[0], dims, preferred_element_type=F32) + lax.dot_general(
            left[1], right[1], dims, preferred_element_type=F32
        )

    def rs_copy(a, d, t, s):
        far = skip and t == 0 and depth(d, s) == 4
        sub = pl.ds(0, srow + (EXTRA if s == 0 else 0))
        return remote(
            rs_s.at[a, d, t, s, sub], rs_r.at[a, d, t, s, sub], rs_ss.at[a, d, t, s], rs_rs.at[a, d, t, s],
            (ring2 if far else ring)[a][d],
        )

    def takes(d, t, s):
        if skip and depth(d, s) == 4:
            return {0: [], 1: [], 2: [0, 1], 3: [2]}[t]
        return [t - 1] if t > 0 else []

    def add_in(a, d, s, value, carried, messages):
        for m in messages:
            rs_copy(a, d, m, s).wait_recv()
            value = value + rs_r[a, d, m, s, :srow].astype(F32)
            if s == 0:
                got = join_rows(rs_r[a, d, m, s, srow:], 2)
                carried = [u + w for u, w in zip(carried, got)]
        return value, carried

    def rs_send(a, d, t, s):
        block = ring_block(a, 1 - d, depth(d, s) - t)
        value, carried = add_in(a, d, s, product(a, block, s), ring_extra[a], takes(d, t, s))
        rs_s[a, d, t, s, :srow] = value.astype(BF16)
        if s == 0:
            rs_s[a, d, t, s, srow:] = split_rows(carried, width)
        go(rs_copy(a, d, t, s))

    lanes = [(s, a, d) for s in range(STREAMS) for a in range(2) for d in range(2)]
    for step in range(half):
        for s, a, d in lanes:
            deep = depth(d, s)
            if skip and deep == 4:
                for t in ([0, 1], [2], [3], [])[step]:
                    rs_send(a, d, t, s)
            elif step < deep:
                rs_send(a, d, step, s)

    def finish(a, s):
        value, carried = product(a, pos[a], s), ring_extra[a]
        for d in range(2):
            if depth(d, s) > 0:
                value, carried = add_in(a, d, s, value, carried, [depth(d, s) - 1])
        return value, carried

    for s in range(STREAMS):
        value, carried = finish(1, s)
        ti_s[pl.ds(s * n // STREAMS, n // STREAMS)] = value.astype(BF16).reshape(n // STREAMS, part_rows, width)
        if s == 0:
            trace2, loss_row = carried
    come_back = Exchange(lambda k: ti_s.at[k], hop_b, lambda k: ti_r.at[part(k)], ti_sem, False)
    come_back.start()
    tr_s[...] = stack_rows([trace2], width)
    swap_tr = Swap(tr_s, tr_r, tr_sem)
    swap_tr.start()
    swap_st.wait_recv()
    far_center, far_inv = tst_r[0:1], tst_r[1:2]
    second = ((own2[...].astype(F32) - far_center) * far_inv).astype(BF16)
    own2[...] = second
    come_back.pass_on([0] + nearest)
    ls_s[...] = jnp.zeros((8, width), F32) + loss_row
    lc = [remote(ls_s, ls_r.at[k], ls_sem.at[0, k], ls_sem.at[1, k], to) for k, to in enumerate(y_peers)]
    for cp in lc:
        go(cp)
    for s in range(STREAMS):
        value, carried = finish(0, s)
        if s == 0:
            trace1, diag_grad = carried
        value = value + own2[stream(s)].astype(F32) * diag_grad - n1f[c, y, stream(s)].astype(F32) * trace1
        g1_o[stream(s)] = (LOSS_SCALE * value * inv1).astype(BF16)
    for cp in late:
        cp.wait_send()
    for cp in lc:
        cp.wait_recv()
    for k in range(n - 1):
        loss_row = loss_row + ls_r[k, 0:1]
    loss_o[...] = loss_row[:, 0:1]
    swap_tr.wait_recv()
    trace2 = tr_r[0:1]
    come_back.wait_recv()
    value = ti_r[...].astype(F32) + n1f[c, y].astype(F32) * diag_grad - own2[...].astype(F32) * trace2
    g2_o[...] = (LOSS_SCALE * value * far_inv).astype(BF16)
    come_back.wait_send()
    swap_tr.wait_send()


def on_device(xs, n, view_one, view_two):
    rows, width = view_one.shape
    half = n // 2
    srow = rows // STREAMS
    prow = width // xs
    sem = pltpu.SemaphoreType.DMA
    blocks = (2, n, rows, width)
    ring = (2, 2, half, STREAMS)
    loss, grad_one, grad_two = pl.pallas_call(
        functools.partial(kernel, xs, n),
        out_shape=(
            jax.ShapeDtypeStruct((1, 1), F32),
            jax.ShapeDtypeStruct((rows, width), BF16),
            jax.ShapeDtypeStruct((rows, width), BF16),
        ),
        in_specs=[pl.BlockSpec(memory_space=pl.ANY)] * 2,
        out_specs=[pl.BlockSpec(memory_space=pltpu.VMEM)] * 3,
        scratch_shapes=[
            pltpu.VMEM(blocks, BF16),
            pltpu.VMEM(blocks, BF16),
            pltpu.VMEM(blocks, BF16),
            pltpu.VMEM(blocks, BF16),
            pltpu.VMEM((rows, width), BF16),
            pltpu.VMEM((n, rows // n, width), BF16),
            pltpu.VMEM((n, rows // n, width), BF16),
            pltpu.VMEM((2, 2, 8, width), F32),
            pltpu.VMEM((2, 2, 8, width), F32),
            pltpu.VMEM((8, width), F32),
            pltpu.VMEM((8, width), F32),
            pltpu.VMEM((8, width), F32),
            pltpu.VMEM((8, width), F32),
            pltpu.VMEM((2, width, width), F32),
            pltpu.VMEM((xs, 2, prow + EXTRA, width), BF16),
            pltpu.VMEM((xs - 1, 2, prow + EXTRA, width), BF16),
            pltpu.VMEM((xs, 2, prow + EXTRA, width), BF16),
            pltpu.VMEM((2, width, width), BF16),
            pltpu.VMEM((width + EXTRA, width), BF16),
            pltpu.VMEM((width + EXTRA, width), BF16),
            pltpu.VMEM(ring + (srow + EXTRA, width), BF16),
            pltpu.VMEM(ring + (srow + EXTRA, width), BF16),
            pltpu.VMEM((n, rows // n, width), BF16),
            pltpu.VMEM((rows, width), BF16),
            pltpu.VMEM((8, width), F32),
            pltpu.VMEM((n - 1, 8, width), F32),
            sem((2,)),
            sem((4, n)),
            sem((2,)),
            sem((2,)),
            sem(ring),
            sem(ring),
            sem((2, n + 1, STREAMS)),
            sem((2, n + 1, STREAMS)),
            sem((2, xs - 1)),
            sem((2, xs - 1)),
            sem((2,)),
            sem(ring),
            sem(ring),
            sem((4, n)),
            sem((2, n - 1)),
        ],
        compiler_params=pltpu.CompilerParams(
            collective_id=0, has_side_effects=True, vmem_limit_bytes=40 * 2**20
        ),
        name="barlow",
    )(view_one, view_two)
    return loss.reshape(()), grad_one, grad_two


def solution(mesh):
    n = mesh.shape["feat"] // 2
    xs = mesh.shape["batch"] // n
    spec = P("batch", "feat")
    return jax.shard_map(
        functools.partial(on_device, xs, n),
        mesh=mesh,
        in_specs=(spec, spec),
        out_specs=(P(), spec, spec),
        check_vma=False,
    )
```

time: 106 us -> 94.4 us (0.89)
  the two profiles are of different devices: /device:TPU:1 before, /device:TPU:8 now
where the time goes in v2:
time: 94.4 us; the launch traced here: 94.2 us
  Pallas kernels  88.7 us (94%)
  local copies, waits for them, and re-layouts  3.11 us (3%)
  between operations  2.41 us (3%)
    pallas_call x1, Pallas kernels, on_device(): pl.pallas_call(functools.partial(kernel, xs, n), out_shape=(jax.ShapeDtyp...  88.7 us
    unnamed x6, local copies, waits for them, and re-layouts  3.11 us

profile of v2, /device:TPU:8, one launch (start us, length us, event | category | flops | bytes accessed | tf_op | source)
XLA Modules:
  0.0 94.2 jit_solution(1367741226090663153)
XLA Ops:
  0.6 0.0 copy-start
  0.6 0.9 copy-done
  1.5 0.0 copy-start.1
  1.5 0.9 copy-done.1
  2.4 88.7 %barlow.1 = (f32[1,1]{1,0:T(1,128)}, bf16[256,256]{1,0:T(8,128)(2,1)S(1)}, bf16[256,256]{1,0:T(8,128)(2,1)S(1)}) custom-call(bf16[256,256]{1,0:T(8,128)(2,1)S(1)} %copy-done, bf16[256,256]{1,0:T(8,128)(2,1)S(1)} %copy-done.1), custom_call_target="tpu_custom_call" | custom-call | tf_op jit(solution)/shard_map/barlow/pallas_call | solution.py:594
  91.7 0.7 copy.9
  92.4 0.7 copy.10
Async XLA Ops:
  0.6 0.9 copy-start
  1.5 0.9 copy-start.1

commit v3 on v2

--- a/solution.py
+++ b/solution.py
@@ -45,7 +45,7 @@
 def kernel(
     xs, n, v1, v2, loss_o, g1_o, g2_o,
     raw1, raw2, n1f, n2f, own2, hop_a, hop_b, ssum, qsum, tst_s, tst_r, tr_s, tr_r,
-    acc, pst, pr, gx, gfull, sib_s, sib_r,
+    acc, pst, pr, gx, gfull, gother, sib_r,
     rs_s, rs_r, ti_s, ti_r, ls_s, ls_r,
     in_sem, t_sem, tst_sem, tr_sem, ag_ss, ag_rs, sb_ss, sb_rs,
     px_sem, gx_sem, sib_sem, rs_ss, rs_rs, ti_sem, ls_sem,
@@ -55,6 +55,7 @@
     srow = rows // STREAMS
     prow = width // xs
     part_rows = rows // n
+    home = n // 4
     group_rows = float(rows * n)
     total_rows = float(rows * n * xs)
     b, f = lax.axis_index("batch"), lax.axis_index("feat")
@@ -95,7 +96,7 @@
     def stream(s):
         return pl.ds(s * srow, srow)
 
-    load1 = pltpu.make_async_copy(v1, raw1.at[c, y], in_sem.at[0])
+    load1 = pltpu.make_async_copy(v1, raw1.at[c, home], in_sem.at[0])
     load2 = pltpu.make_async_copy(v2, own2, in_sem.at[1])
     load1.start()
     load2.start()
@@ -164,26 +165,26 @@
             self.to = (lambda k: dev(x, k, z, c)) if along_z else (lambda k: dev(x, y, k, c))
 
         def first(self, k):
-            hop_ref = self.hop.at[self.here]
             return remote(
-                self.source(wrap(self.here + k, n)), hop_ref, self.sems.at[0, k], self.sems.at[1, k], self.peers[k - 1]
+                self.source(k), self.hop.at[self.here], self.sems.at[0, k], self.sems.at[1, k], self.peers[k - 1]
             )
 
         def stay(self):
-            return pltpu.make_async_copy(self.source(self.here), self.hop.at[self.here], self.sems.at[1, 0])
+            return pltpu.make_async_copy(self.source(0), self.hop.at[self.here], self.sems.at[1, 0])
 
         def second(self, k):
             origin = wrap(self.here - k, n)
-            far = remote(
-                self.hop.at[origin], self.target(self.there), self.sems.at[2, k], self.sems.at[3, self.there], self.to(origin)
-            )
-            near = pltpu.make_async_copy(self.hop.at[origin], self.target(self.there), self.sems.at[3, self.there])
+            src, sem = self.hop.at[origin], self.sems.at[3, self.there]
+            far = remote(src, self.target(wrap(self.there - origin, n), origin), self.sems.at[2, k], sem, self.to(origin))
+            near = pltpu.make_async_copy(src, self.target(0, self.there), sem)
             return origin, far, near
 
-        def start(self):
-            self.stay().start()
-            for k in nearest:
-                self.first(k).start()
+        def start(self, some):
+            for k in some:
+                if k == 0:
+                    self.stay().start()
+                else:
+                    self.first(k).start()
 
         def pass_on(self, some):
             for k in some:
@@ -201,14 +202,13 @@
                 def _():
                     near.start()
 
-        def wait_recv(self):
-            for k in [0] + nearest:
-                came = wrap(self.there + k, n)
-                ref = self.target(came)
+        def wait_recv(self, some):
+            for k in some:
+                ref, sem = self.target(k, self.there), self.sems.at[3, wrap(self.there + k, n)]
                 if k == 0:
-                    pltpu.make_async_copy(ref, ref, self.sems.at[3, came]).wait()
+                    pltpu.make_async_copy(ref, ref, sem).wait()
                 else:
-                    remote(ref, ref, self.sems.at[2, k], self.sems.at[3, came], self.peers[0]).wait_recv()
+                    remote(ref, ref, self.sems.at[2, k], sem, self.peers[0]).wait_recv()
 
         def wait_send(self):
             for k in nearest:
@@ -220,8 +220,11 @@
                 def _():
                     far.wait_send()
 
-    spread_out = Exchange(lambda k: own2.at[part(k)], hop_a, lambda k: raw2.at[c, k, part(z)], t_sem, True)
-    spread_out.start()
+    every_k = [0] + nearest
+    spread_out = Exchange(
+        lambda k: own2.at[part(wrap(z + k, n))], hop_a, lambda k, _: raw2.at[c, wrap(home + k, n), part(z)], t_sem, True
+    )
+    spread_out.start(every_k)
 
     raws, norms = (raw1, raw2), (n1f, n2f)
 
@@ -229,6 +232,8 @@
         return half if (s < STREAMS // 2) == (d == 0) else half - 1
 
     def ring_block(a, d, t):
+        if a == 0:
+            return (home + (t if d else -t)) % n
         return wrap(pos[a] - t, n) if d == 0 else wrap(pos[a] + t, n)
 
     def piece(a, core, block, s):
@@ -243,9 +248,10 @@
 
     def ag_copy(a, d, t, s):
         far = skip and t == 3
-        block = ring_block(a, d, 2 if far else t)
-        ref = piece(a, c, block, s)
-        return remote(ref, ref, ag_ss.at[a, d, t, s], ag_rs.at[a, d, t, s], (ring2 if far else ring)[a][d])
+        steps = 2 if far else t
+        src = piece(a, c, ring_block(a, d, steps), s)
+        dst = piece(a, c, ring_block(a, d, steps + (2 if far else 1)), s) if a == 0 else src
+        return remote(src, dst, ag_ss.at[a, d, t, s], ag_rs.at[a, d, t, s], (ring2 if far else ring)[a][d])
 
     def sib_copy(a, core, block, s, slot):
         ref = piece(a, core, block, s)
@@ -258,7 +264,7 @@
         for d in range(2):
             if depth(d, s) > 0:
                 go(ag_copy(a, d, 0, s))
-        go(sib_copy(a, c, pos[a], s, 0))
+        go(sib_copy(a, c, ring_block(a, 0, 0), s, 0))
 
     def forward(a, t):
         for s in range(STREAMS):
@@ -274,7 +280,7 @@
 
     def sib_wait(a, s, d, t):
         if d is None:
-            sib_copy(a, o, pos[a], s, 0).wait_recv()
+            sib_copy(a, o, ring_block(a, 0, 0), s, 0).wait_recv()
         elif t < depth(d, s):
             sib_copy(a, o, ring_block(a, d, t + 1), s, ring_slot(d, t)).wait_recv()
 
@@ -310,43 +316,49 @@
             else:
                 acc[h] += share
 
+    def blocks_of(a, t):
+        if t + 1 < half:
+            return [ring_block(a, 0, t + 1), ring_block(a, 1, t + 1)]
+        return [ring_block(a, 0, half)]
+
     def arrived(a, t):
-        if t + 1 < half:
-            blocks = [ring_block(a, 0, t + 1), ring_block(a, 1, t + 1)]
-        else:
-            blocks = [ring_block(a, 0, half)]
         for s in range(STREAMS):
             for d in range(2):
                 sib_wait(a, s, d, t)
-        for block in blocks:
+        for block in blocks_of(a, t):
             shifted(a, block, False)
-            if a == 1:
-                correlate(block, False)
+
+    def correlate_all(t):
+        for block in blocks_of(1, t):
+            correlate(block, False)
 
     for s in range(STREAMS):
         open_ring(0, s)
-    spread_out.pass_on([0] + nearest)
-    spread_out.wait_recv()
+    spread_out.pass_on(every_k)
     for s in range(STREAMS):
+        spread_out.wait_recv([k for k in every_k if (home + k) % n * STREAMS // n == s])
         open_ring(1, s)
+    forward(0, 0)
     for s in range(STREAMS):
         sib_wait(0, s, None, 0)
-    shifted(0, y, True)
-    forward(0, 0)
-    forward(1, 0)
     for s in range(STREAMS):
         sib_wait(1, s, None, 0)
+    shifted(0, home, True)
     shifted(1, z, True)
     for t in range(1, half):
+        forward(1, t - 1)
         forward(0, t)
-        forward(1, t)
         arrived(0, t - 1)
-        if t == 1 and half > 1:
-            pass
+        if t > 1:
+            arrived(1, t - 2)
     arrived(0, half - 1)
     correlate(z, True)
-    for t in range(half):
+    for t in range(half - 2):
+        correlate_all(t)
+    forward(1, half - 1)
+    for t in range(max(half - 2, 0), half):
         arrived(1, t)
+        correlate_all(t)
 
     def spread(row, count, first):
         ids = lax.broadcasted_iota(jnp.int32, (count, width), 0) + first
@@ -437,10 +449,15 @@
     row_trace = jnp.sum(jnp.where(same, row_trace, 0.0), axis=0, keepdims=True)
     loss_row = jnp.zeros((1, width), F32) + loss
     gx[x, 0, prow:] = split_rows([col_trace[0], row_trace, loss_row], width)
-    gx[x, 1, prow:] = split_rows([col_trace[1]], width)
+    gx[x, 1, prow:] = split_rows([col_trace[1], row_trace, loss_row], width)
     gc = [remote(gx.at[x], gx.at[x], gx_sem.at[0, k], gx_sem.at[1, k], to) for k, to in enumerate(x_peers)]
     for cp in gc:
         cp.start()
+
+    def over(k):
+        return remote(gx.at[k, o], sib_r.at[k], sib_sem.at[0, k], sib_sem.at[1, k], sibling)
+
+    over(x).start()
 
     def standard(i, _):
         n1f[c, i] = ((raw1[c, i].astype(F32) - center1) * inv1).astype(BF16)
@@ -457,6 +474,7 @@
     for k in range(1, xs):
         src = wrap(x - k, xs)
         remote(gx.at[src], gx.at[src], gx_sem.at[0, k - 1], gx_sem.at[1, k - 1], x_peers[k - 1]).wait_recv()
+        over(src).start()
     col0 = col1 = trace1 = loss_row = jnp.zeros((1, width), F32)
     for k in range(xs):
         for h in range(2):
@@ -464,21 +482,17 @@
         got = join_rows(gx[k, 0, prow:], 3)
         col0, trace1, loss_row = col0 + got[0], trace1 + got[1], loss_row + got[2]
         col1 = col1 + join_rows(gx[k, 1, prow:], 1)[0]
-    mine = jnp.where(is_low, col0, col1)
-    theirs = jnp.where(is_low, col1, col0)
     diag_trace = diag * diag_grad
     trace1 = trace1 + diag_trace
-    trace2 = mine + diag_trace
-
-    sib_s[:width] = gfull[o]
-    sib_s[width:] = split_rows([theirs, loss_row], width)
-    sib = remote(sib_s, sib_r, sib_sem.at[0], sib_sem.at[1], sibling)
-    sib.start()
-    late = gc + [sib]
-    sib.wait_recv()
-    got = join_rows(sib_r[width:], 2)
-    trace2 = trace2 + got[0]
-    loss_row = loss_row + got[1]
+    trace2 = jnp.where(is_low, col0, col1) + diag_trace
+    late = gc
+    for k in range(xs):
+        over(k).wait_recv()
+    for k in range(xs):
+        gother[k * prow : (k + 1) * prow] = sib_r[k, :prow]
+        got = join_rows(sib_r[k, prow:], 3)
+        trace2 = trace2 + got[0]
+        loss_row = loss_row + got[2]
 
     ring_extra = [[trace1, diag_grad], [trace2, loss_row]]
 
@@ -490,7 +504,7 @@
             dims = (((1,), (0,)), ((), ()))
             images = pl.ds(s * n // STREAMS, n // STREAMS)
             left = [n1f[h, images, part(block)].reshape(srow, width) for h in (c, o)]
-            right = (gfull[c], sib_r[:width])
+            right = (gfull[c], gother[...])
         return lax.dot_general(left[0], right[0], dims, preferred_element_type=F32) + lax.dot_general(
             left[1], right[1], dims, preferred_element_type=F32
         )
@@ -525,7 +539,7 @@
             rs_s[a, d, t, s, srow:] = split_rows(carried, width)
         go(rs_copy(a, d, t, s))
 
-    lanes = [(s, a, d) for s in range(STREAMS) for a in range(2) for d in range(2)]
+    lanes = [(s, a, d) for s in reversed(range(STREAMS)) for a in (1, 0) for d in range(2)]
     for step in range(half):
         for s, a, d in lanes:
             deep = depth(d, s)
@@ -536,19 +550,21 @@
                 rs_send(a, d, step, s)
 
     def finish(a, s):
-        value, carried = product(a, pos[a], s), ring_extra[a]
+        value, carried = product(a, ring_block(a, 0, 0), s), ring_extra[a]
         for d in range(2):
             if depth(d, s) > 0:
                 value, carried = add_in(a, d, s, value, carried, [depth(d, s) - 1])
         return value, carried
 
-    for s in range(STREAMS):
+    come_back = Exchange(
+        lambda k: ti_s.at[(home + k) % n], hop_b, lambda k, base: ti_r.at[part(wrap(base + k, n))], ti_sem, False
+    )
+    for s in reversed(range(STREAMS)):
         value, carried = finish(1, s)
         ti_s[pl.ds(s * n // STREAMS, n // STREAMS)] = value.astype(BF16).reshape(n // STREAMS, part_rows, width)
         if s == 0:
             trace2, loss_row = carried
-    come_back = Exchange(lambda k: ti_s.at[k], hop_b, lambda k: ti_r.at[part(k)], ti_sem, False)
-    come_back.start()
+        come_back.start([k for k in reversed(every_k) if (home + k) % n * STREAMS // n == s])
     tr_s[...] = stack_rows([trace2], width)
     swap_tr = Swap(tr_s, tr_r, tr_sem)
     swap_tr.start()
@@ -556,7 +572,7 @@
     far_center, far_inv = tst_r[0:1], tst_r[1:2]
     second = ((own2[...].astype(F32) - far_center) * far_inv).astype(BF16)
     own2[...] = second
-    come_back.pass_on([0] + nearest)
+    come_back.pass_on(every_k)
     ls_s[...] = jnp.zeros((8, width), F32) + loss_row
     lc = [remote(ls_s, ls_r.at[k], ls_sem.at[0, k], ls_sem.at[1, k], to) for k, to in enumerate(y_peers)]
     for cp in lc:
@@ -565,10 +581,12 @@
         value, carried = finish(0, s)
         if s == 0:
             trace1, diag_grad = carried
-        value = value + own2[stream(s)].astype(F32) * diag_grad - n1f[c, y, stream(s)].astype(F32) * trace1
+        value = value + own2[stream(s)].astype(F32) * diag_grad - n1f[c, home, stream(s)].astype(F32) * trace1
         g1_o[stream(s)] = (LOSS_SCALE * value * inv1).astype(BF16)
     for cp in late:
         cp.wait_send()
+    for k in range(xs):
+        over(k).wait_send()
     for cp in lc:
         cp.wait_recv()
     for k in range(n - 1):
@@ -576,8 +594,8 @@
     loss_o[...] = loss_row[:, 0:1]
     swap_tr.wait_recv()
     trace2 = tr_r[0:1]
-    come_back.wait_recv()
-    value = ti_r[...].astype(F32) + n1f[c, y].astype(F32) * diag_grad - own2[...].astype(F32) * trace2
+    come_back.wait_recv(every_k)
+    value = ti_r[...].astype(F32) + n1f[c, home].astype(F32) * diag_grad - own2[...].astype(F32) * trace2
     g2_o[...] = (LOSS_SCALE * value * far_inv).astype(BF16)
     come_back.wait_send()
     swap_tr.wait_send()
@@ -598,7 +616,7 @@
             jax.ShapeDtypeStruct((rows, width), BF16),
             jax.ShapeDtypeStruct((rows, width), BF16),
         ),
-        in_specs=[pl.BlockSpec(memory_space=pl.ANY)] * 2,
+        in_specs=[pl.BlockSpec(memory_space=pltpu.HBM)] * 2,
         out_specs=[pl.BlockSpec(memory_space=pltpu.VMEM)] * 3,
         scratch_shapes=[
             pltpu.VMEM(blocks, BF16),
@@ -619,8 +637,8 @@
             pltpu.VMEM((xs - 1, 2, prow + EXTRA, width), BF16),
             pltpu.VMEM((xs, 2, prow + EXTRA, width), BF16),
             pltpu.VMEM((2, width, width), BF16),
-            pltpu.VMEM((width + EXTRA, width), BF16),
-            pltpu.VMEM((width + EXTRA, width), BF16),
+            pltpu.VMEM((width, width), BF16),
+            pltpu.VMEM((xs, prow + EXTRA, width), BF16),
             pltpu.VMEM(ring + (srow + EXTRA, width), BF16),
             pltpu.VMEM(ring + (srow + EXTRA, width), BF16),
             pltpu.VMEM((n, rows // n, width), BF16),
@@ -637,14 +655,14 @@
             sem((2, n + 1, STREAMS)),
             sem((2, xs - 1)),
             sem((2, xs - 1)),
-            sem((2,)),
+            sem((2, xs)),
             sem(ring),
             sem(ring),
             sem((4, n)),
             sem((2, n - 1)),
         ],
         compiler_params=pltpu.CompilerParams(
-            collective_id=0, has_side_effects=True, vmem_limit_bytes=40 * 2**20
+            collective_id=0, has_side_effects=True, vmem_limit_bytes=60 * 2**20
         ),
         name="barlow",
     )(view_one, view_two)

time: 94.4 us -> 88.2 us (0.934)
  the two profiles are of different devices: /device:TPU:8 before, /device:TPU:1 now
where the time goes in v3:
time: 88.2 us; the launch traced here: 88 us
  Pallas kernels  83.4 us (95%)
  between operations  2.32 us (3%)
  local copies, waits for them, and re-layouts  2.26 us (3%)
    pallas_call x1, Pallas kernels, on_device(): pl.pallas_call(functools.partial(kernel, xs, n), out_shape=(jax.ShapeDtyp...  83.4 us
    unnamed x4, local copies, waits for them, and re-layouts  2.26 us

profile of v3, /device:TPU:1, one launch (start us, length us, event | category | flops | bytes accessed | tf_op | source)
XLA Modules:
  0.0 88.0 jit_solution(2726371310545634782)
XLA Ops:
  0.6 83.4 %barlow.1 = (f32[1,1]{1,0:T(1,128)}, bf16[256,256]{1,0:T(8,128)(2,1)}, bf16[256,256]{1,0:T(8,128)(2,1)}) custom-call(bf16[256,256]{1,0:T(8,128)(2,1)} %v1.1, bf16[256,256]{1,0:T(8,128)(2,1)} %v2.1), custom_call_target="tpu_custom_call" | custom-call | tf_op jit(solution)/shard_map/barlow/pallas_call | solution.py:612
  84.6 0.0 copy-start
  84.6 1.6 %copy.9 = bf16[256,256]{1,0:T(8,128)(2,1)} copy(bf16[256,256]{1,0:T(8,128)(2,1)} %get-tuple-element.13) | data formatting | bytes 262144
  86.2 0.0 copy-done
  86.2 0.7 copy.10
Async XLA Ops:
  84.6 1.6 %copy-start = (bf16[256,256]{1,0:T(8,128)(2,1)S(1)}, bf16[256,256]{1,0:T(8,128)(2,1)}, u32[]{:S(2)}) copy-start(bf16[256,256]{1,0:T(8,128)(2,1)} %get-tuple-element.14) | copy-start | bytes 393220

commit v4 on v3

--- a/solution.py
+++ b/solution.py
@@ -224,7 +224,7 @@
     spread_out = Exchange(
         lambda k: own2.at[part(wrap(z + k, n))], hop_a, lambda k, _: raw2.at[c, wrap(home + k, n), part(z)], t_sem, True
     )
-    spread_out.start(every_k)
+    spread_out.start(every_k[::-1])
 
     raws, norms = (raw1, raw2), (n1f, n2f)
 
@@ -397,7 +397,7 @@
         remote(pst.at[wrap(x + k, xs)], pr.at[k - 1], px_sem.at[0, k - 1], px_sem.at[1, k - 1], x_peers[k - 1])
         for k in range(1, xs)
     ]
-    for cp in px:
+    for cp in px[1:2] + px[:1] + px[2:]:
         go(cp)
     for cp in px:
         cp.wait_recv()
@@ -451,7 +451,7 @@
     gx[x, 0, prow:] = split_rows([col_trace[0], row_trace, loss_row], width)
     gx[x, 1, prow:] = split_rows([col_trace[1], row_trace, loss_row], width)
     gc = [remote(gx.at[x], gx.at[x], gx_sem.at[0, k], gx_sem.at[1, k], to) for k, to in enumerate(x_peers)]
-    for cp in gc:
+    for cp in gc[1:2] + gc[:1] + gc[2:]:
         cp.start()
 
     def over(k):

time: 88.2 us -> 87.5 us (level)
  Pallas kernels: 83.4 us -> 82 us
    pallas_call x1, Pallas kernels: 83.4 us -> 82 us  [on_device(): pl.pallas_call(functools.partial(kernel, xs, n), out_shape=(jax.ShapeDtyp...]
where the time goes in v4:
time: 87.5 us; the launch traced here: 86.5 us
  Pallas kernels  82 us (94%)
  between operations  2.32 us (3%)
  local copies, waits for them, and re-layouts  2.26 us (3%)
    pallas_call x1, Pallas kernels, on_device(): pl.pallas_call(functools.partial(kernel, xs, n), out_shape=(jax.ShapeDtyp...  82 us
    unnamed x4, local copies, waits for them, and re-layouts  2.26 us

profile of v4, /device:TPU:1, one launch (start us, length us, event | category | flops | bytes accessed | tf_op | source)
XLA Modules:
  0.0 86.5 jit_solution(18312769296326837476)
XLA Ops:
  0.6 82.0 %barlow.1 = (f32[1,1]{1,0:T(1,128)}, bf16[256,256]{1,0:T(8,128)(2,1)}, bf16[256,256]{1,0:T(8,128)(2,1)}) custom-call(bf16[256,256]{1,0:T(8,128)(2,1)} %v1.1, bf16[256,256]{1,0:T(8,128)(2,1)} %v2.1), custom_call_target="tpu_custom_call" | custom-call | tf_op jit(solution)/shard_map/barlow/pallas_call | solution.py:612
  83.1 0.0 copy-start
  83.1 1.6 %copy.9 = bf16[256,256]{1,0:T(8,128)(2,1)} copy(bf16[256,256]{1,0:T(8,128)(2,1)} %get-tuple-element.13) | data formatting | bytes 262144
  84.8 0.0 copy-done
  84.8 0.7 copy.10
Async XLA Ops:
  83.1 1.6 %copy-start = (bf16[256,256]{1,0:T(8,128)(2,1)S(1)}, bf16[256,256]{1,0:T(8,128)(2,1)}, u32[]{:S(2)}) copy-start(bf16[256,256]{1,0:T(8,128)(2,1)} %get-tuple-element.14) | copy-start | bytes 393220

commit v5 on v4

--- a/solution.py
+++ b/solution.py
@@ -572,17 +572,17 @@
     far_center, far_inv = tst_r[0:1], tst_r[1:2]
     second = ((own2[...].astype(F32) - far_center) * far_inv).astype(BF16)
     own2[...] = second
-    come_back.pass_on(every_k)
-    ls_s[...] = jnp.zeros((8, width), F32) + loss_row
-    lc = [remote(ls_s, ls_r.at[k], ls_sem.at[0, k], ls_sem.at[1, k], to) for k, to in enumerate(y_peers)]
-    for cp in lc:
-        go(cp)
     for s in range(STREAMS):
         value, carried = finish(0, s)
         if s == 0:
             trace1, diag_grad = carried
         value = value + own2[stream(s)].astype(F32) * diag_grad - n1f[c, home, stream(s)].astype(F32) * trace1
         g1_o[stream(s)] = (LOSS_SCALE * value * inv1).astype(BF16)
+    come_back.pass_on(every_k)
+    ls_s[...] = jnp.zeros((8, width), F32) + loss_row
+    lc = [remote(ls_s, ls_r.at[k], ls_sem.at[0, k], ls_sem.at[1, k], to) for k, to in enumerate(y_peers)]
+    for cp in lc:
+        go(cp)
     for cp in late:
         cp.wait_send()
     for k in range(xs):

time: 87.5 us -> 87.5 us (level)
  no operation moved by 1% of the time
where the time goes in v5:
time: 87.5 us; the launch traced here: 86.7 us
  Pallas kernels  82.2 us (94%)
  between operations  2.32 us (3%)
  local copies, waits for them, and re-layouts  2.26 us (3%)
    pallas_call x1, Pallas kernels, on_device(): pl.pallas_call(functools.partial(kernel, xs, n), out_shape=(jax.ShapeDtyp...  82.2 us
    unnamed x4, local copies, waits for them, and re-layouts  2.26 us

profile of v5, /device:TPU:1, one launch (start us, length us, event | category | flops | bytes accessed | tf_op | source)
XLA Modules:
  0.0 86.7 jit_solution(3487258793259788003)
XLA Ops:
  0.6 82.2 %barlow.1 = (f32[1,1]{1,0:T(1,128)}, bf16[256,256]{1,0:T(8,128)(2,1)}, bf16[256,256]{1,0:T(8,128)(2,1)}) custom-call(bf16[256,256]{1,0:T(8,128)(2,1)} %v1.1, bf16[256,256]{1,0:T(8,128)(2,1)} %v2.1), custom_call_target="tpu_custom_call" | custom-call | tf_op jit(solution)/shard_map/barlow/pallas_call | solution.py:612
  83.3 0.0 copy-start
  83.4 1.6 %copy.9 = bf16[256,256]{1,0:T(8,128)(2,1)} copy(bf16[256,256]{1,0:T(8,128)(2,1)} %get-tuple-element.13) | data formatting | bytes 262144
  85.0 0.0 copy-done
  85.0 0.7 copy.10
Async XLA Ops:
  83.3 1.6 %copy-start = (bf16[256,256]{1,0:T(8,128)(2,1)S(1)}, bf16[256,256]{1,0:T(8,128)(2,1)}, u32[]{:S(2)}) copy-start(bf16[256,256]{1,0:T(8,128)(2,1)} %get-tuple-element.14) | copy-start | bytes 393220
